TPU v7x, 32 devices: a whole 2x2x4 slice. The times are simulated.
32 devices in a mesh: seq: 8 (over z, y), ch: 4 (over x, core).
Axes of the slice: x: 2, y: 2, z: 4, core: 2. Of those that a mesh axis runs over, the one named last changes fastest.
Arguments:
- query_rows: bfloat16 [2048, 4096], P(('seq', 'ch')), may hold values from -6 to 6
- key_rows: bfloat16 [2048, 4096], P(('seq', 'ch')), may hold values from -6 to 6
- value_rows: bfloat16 [2048, 4096], P(('seq', 'ch')), may hold values from -6 to 6
- filter_taps: float32 [2048, 4096], P(('seq', 'ch')), may hold values from -1.1 to 1.1
- skip_gain: float32 [4096], replicated, may hold values from 0.5 to 1.5
Outputs:
- gated_output: bfloat16 [2048, 4096], P(('seq', 'ch'))
All inputs are finite; a program needn't handle non-finite values.
Results may differ from a plain program's by a relative error of at most 0.0014.
Values sent between devices are 32-bit elements; how exact they have to be, the bound alone decides.
A program may use at most 128 MiB of HBM per device.

v0:
```python
import math

import jax
import jax.numpy as jnp
from jax import lax
from jax.sharding import PartitionSpec as P

highest = lax.Precision.HIGHEST


def angles(product_ids, modulus):
    return 2.0 * math.pi / modulus * (product_ids % modulus).astype(jnp.float32)


def contract(pattern, weights, operand):
    return jnp.einsum(
        pattern, weights, operand, precision=highest, preferred_element_type=jnp.float32
    )


def shards(query_rows, key_rows, value_rows, filter_taps, skip_gain):
    seq_count = lax.axis_size("seq")
    group_count = lax.axis_size("ch")
    position = lax.axis_index("seq")
    row_count, full_width = key_rows.shape
    per_peer = row_count // seq_count
    columns = full_width // group_count
    local_rows = group_count * per_peer
    tokens = row_count * group_count
    slot_count = 2 * seq_count
    length = 2 * tokens * seq_count
    signal = key_rows.astype(jnp.float32) * value_rows.astype(jnp.float32)
    layout = (1, seq_count, 1, per_peer, full_width)
    moved_signal, moved_filter = (
        lax.all_to_all(
            lax.all_to_all(signal.reshape(layout), "seq", split_axis=1, concat_axis=0, tiled=True),
            "ch",
            split_axis=4,
            concat_axis=2,
            tiled=True,
        ),
        lax.all_to_all(
            lax.all_to_all(
                filter_taps.reshape(layout), "seq", split_axis=1, concat_axis=0, tiled=True
            ),
            "ch",
            split_axis=4,
            concat_axis=2,
            tiled=True,
        ),
    )
    moved_signal = moved_signal.reshape(seq_count, local_rows, columns)
    moved_filter = moved_filter.reshape(seq_count, local_rows, columns)
    slot_ids = jnp.arange(slot_count, dtype=jnp.int32)
    owners = slot_ids // 2
    freq_slot = jnp.where(
        slot_ids % 2 == 0, owners, jnp.where(owners == 0, seq_count, slot_count - owners)
    )
    blocks = jnp.arange(seq_count, dtype=jnp.int32)
    block_phase = angles(freq_slot[:, None] * blocks[None, :], slot_count)
    block_cos = jnp.cos(block_phase)
    block_sin = jnp.sin(block_phase)
    local_ids = jnp.arange(local_rows, dtype=jnp.int32)
    local_time = local_ids // per_peer * row_count + position * per_peer + local_ids % per_peer
    twist_angle = -angles(freq_slot[:, None] * local_time[None, :], length)
    twist_cos = jnp.cos(twist_angle)[:, :, None]
    twist_sin = jnp.sin(twist_angle)[:, :, None]

    def forward_blocks(real_part):
        out_real = contract("jd,dmc->jmc", block_cos, real_part)
        out_imag = -contract("jd,dmc->jmc", block_sin, real_part)
        return jnp.stack(
            [
                out_real * twist_cos - out_imag * twist_sin,
                out_real * twist_sin + out_imag * twist_cos,
            ]
        )

    all_ids = jnp.arange(tokens, dtype=jnp.int32)
    peer_id = all_ids // local_rows
    within = all_ids % local_rows
    all_time = within // per_peer * row_count + peer_id * per_peer + within % per_peer
    inner_phase = angles(all_ids[:, None] * all_time[None, :], tokens)
    inner_cos = jnp.cos(inner_phase)
    inner_sin = jnp.sin(inner_phase)

    def forward_inner(spectrum):
        real_part = spectrum[0]
        imag_part = spectrum[1]
        out_real = contract("qp,jpc->jqc", inner_cos, real_part) + contract(
            "qp,jpc->jqc", inner_sin, imag_part
        )
        out_imag = contract("qp,jpc->jqc", inner_cos, imag_part) - contract(
            "qp,jpc->jqc", inner_sin, real_part
        )
        return (out_real, out_imag)

    signal_spectrum, filter_spectrum = (
        lax.all_to_all(
            forward_blocks(moved_signal), "seq", split_axis=1, concat_axis=2, tiled=True
        ),
        lax.all_to_all(
            forward_blocks(moved_filter), "seq", split_axis=1, concat_axis=2, tiled=True
        ),
    )
    signal_real, signal_imag = forward_inner(signal_spectrum)
    filter_real, filter_imag = forward_inner(filter_spectrum)
    product_real = signal_real * filter_real - signal_imag * filter_imag
    product_imag = signal_real * filter_imag + signal_imag * filter_real
    back_real = contract("qp,jqc->jpc", inner_cos, product_real) - contract(
        "qp,jqc->jpc", inner_sin, product_imag
    )
    back_imag = contract("qp,jqc->jpc", inner_cos, product_imag) + contract(
        "qp,jqc->jpc", inner_sin, product_real
    )
    my_slots = jnp.stack([position, jnp.where(position == 0, seq_count, slot_count - position)])
    back_phase = angles(my_slots[:, None] * all_time[None, :], length)[:, :, None]
    back_cos = jnp.cos(back_phase)
    back_sin = jnp.sin(back_phase)
    turned_real = back_real * back_cos - back_imag * back_sin
    turned_imag = back_real * back_sin + back_imag * back_cos
    inverse_scale = 1.0 / length
    gathered = lax.all_to_all(
        jnp.stack([turned_real, turned_imag]), "seq", split_axis=2, concat_axis=1, tiled=True
    )
    convolved = (
        contract("jd,jmc->dmc", block_cos, gathered[0])
        - contract("jd,jmc->dmc", block_sin, gathered[1])
    ) * inverse_scale
    returned = lax.all_to_all(
        lax.all_to_all(
            convolved.reshape(seq_count, 1, group_count, per_peer, columns),
            "seq",
            split_axis=0,
            concat_axis=1,
            tiled=True,
        ),
        "ch",
        split_axis=2,
        concat_axis=4,
        tiled=True,
    )
    convolved_rows = returned.reshape(row_count, full_width)
    gated = query_rows.astype(jnp.float32) * (convolved_rows + skip_gain[None, :] * signal)
    return gated.astype(jnp.bfloat16)


def solution(mesh):
    in_specs = (
        P(("seq", "ch"), None),
        P(("seq", "ch"), None),
        P(("seq", "ch"), None),
        P(("seq", "ch"), None),
        P(),
    )
    out_specs = P(("seq", "ch"), None)
    return jax.shard_map(shards, mesh=mesh, in_specs=in_specs, out_specs=out_specs, check_vma=False)
```

profile of v0, /device:TPU:31, one launch (start us, length us, event | category | flops | bytes accessed | tf_op | source)
XLA Modules:
  0.0 573.0 jit_solution(11160475574549039905)
XLA Ops:
  0.0 5.6 all-to-all-start.3
  5.6 1.1 fusion.15
  6.7 23.0 %all-to-all-done.3 = f32[1,8,1,8,4096]{4,3,2,0,1:T(8,128)S(1)} async-done(((f32[1,8,1,8,4096]{4,3,2,0,1:T(8,128)}), f32[1,8,1,8,4096]{4,3,2,0,1:T(8,128)S(1)}, u32[]{:S(2)}, u32[]{:S(2)}) %all-to-all-start.3) | async-done | bytes 1048608 | tf_op jit(solution)/shard_map/all_to_all | solution.py:43
  29.7 5.4 all-to-all-start
  35.1 8.7 %copy.61 = f32[8,1,1,8,4096]{3,0,2,1,4:T(8,128)} copy(f32[8,1,1,8,4096]{4,3,0,2,1:T(8,128)S(1)} %bitcast.159) | data formatting | bytes 2097152 | tf_op jit(solution)/shard_map/all_to_all | solution.py:43
  43.8 11.9 %reshape.292 = f32[4,1,65536]{2,1,0:T(1,128)} reshape(f32[4096,1,1,8,8]{4,3,2,1,0:T(8,128)} %bitcast.139) | data formatting | bytes 2097152
  55.7 3.5 all-to-all-done
  59.3 4.2 all-to-all-start.4
  63.4 8.7 %copy.52 = f32[8,1,1,8,4096]{3,0,2,1,4:T(8,128)} copy(f32[8,1,1,8,4096]{4,3,0,2,1:T(8,128)S(1)} %bitcast.158) | data formatting | bytes 2097152 | tf_op jit(solution)/shard_map/all_to_all | solution.py:36
  72.2 11.9 %reshape.290 = f32[4,1,65536]{2,1,0:T(1,128)} reshape(f32[4096,1,1,8,8]{4,3,2,1,0:T(8,128)} %bitcast.140) | data formatting | bytes 2097152
  84.1 4.7 all-to-all-start.1
  89.5 3.7 reduce
  93.2 14.8 %reshape.293 = f32[4096,1,1,8,8]{4,3,2,1,0:T(8,128)} reshape(f32[4,65536]{1,0:T(4,128)S(1)} %reduce) | data formatting | bytes 2097152
  108.0 10.0 %copy.90 = f32[8,1,1,8,4,1024]{5,4,3,0,2,1:T(4,128)S(1)} copy(f32[8,1,1,8,4,1024]{3,0,5,4,2,1:T(8,128)} %bitcast.141) | data formatting | bytes 2097152 | tf_op jit(solution)/shard_map/all_to_all | solution.py:42
  118.0 0.6 copy.63
  118.6 1.9 fusion.62
  120.5 3.2 fusion.68
  123.7 4.6 reduce.1
  128.3 15.0 %reshape.291 = f32[4096,1,1,8,8]{4,3,2,1,0:T(8,128)} reshape(f32[4,65536]{1,0:T(4,128)S(1)} %reduce.1) | data formatting | bytes 2097152
  143.4 9.8 %copy.89 = f32[8,1,1,8,4,1024]{5,4,3,0,2,1:T(4,128)S(1)} copy(f32[8,1,1,8,4,1024]{3,0,5,4,2,1:T(8,128)} %bitcast.142) | data formatting | bytes 2097152 | tf_op jit(solution)/shard_map/all_to_all | solution.py:35
  153.2 0.6 copy.54
  153.8 1.9 fusion.64
  155.7 4.8 subtract_bitcast_fusion.1
  161.1 4.4 copy.64
  165.6 6.7 %all-to-all-start.5 = ((f32[2,16,32,1024]{3,2,0,1:T(8,128)}), f32[2,16,32,1024]{3,2,0,1:T(8,128)}, u32[]{:S(2)}, u32[]{:S(2)}) async-start(f32[2,16,32,1024]{3,2,0,1:T(8,128)} %copy.64), calls=%async_computation.5 | async-start | bytes 8388608 | tf_op jit(solution)/shard_map/all_to_all | solution.py:102
  172.3 2.0 pad_maximum_fusion
  174.3 4.4 copy.55
  178.7 85.2 %all-to-all-done.5 = f32[2,16,32,1024]{3,2,0,1:T(8,128)} async-done(((f32[2,16,32,1024]{3,2,0,1:T(8,128)}), f32[2,16,32,1024]{3,2,0,1:T(8,128)}, u32[]{:S(2)}, u32[]{:S(2)}) %all-to-all-start.5) | async-done | bytes 4194336 | tf_op jit(solution)/shard_map/all_to_all | solution.py:102
  263.9 6.3 %all-to-all-start.2 = ((f32[2,16,32,1024]{3,2,0,1:T(8,128)}), f32[2,16,32,1024]{3,2,0,1:T(8,128)}, u32[]{:S(2)}, u32[]{:S(2)}) async-start(f32[2,16,32,1024]{3,2,0,1:T(8,128)} %copy.55), calls=%async_computation.2 | async-start | bytes 8388608 | tf_op jit(solution)/shard_map/all_to_all | solution.py:99
  270.4 2.5 copy.65
  272.9 0.6 fusion.169
  274.0 4.4 fusion.31
  278.4 5.8 %fusion.27 = f32[2,1024,256]{2,1,0:T(8,128)} fusion(f32[2,256,1024]{2,1,0:T(8,128)S(1)} %bitcast.145, s32[256]{0:T(256)S(1)} %fusion.88), kind=kOutput, calls=%fused_computation.45 | convolution fusion | flops 1611530240 | bytes 4195328 | tf_op jit(solution)/shard_map/qp,jpc->jqc/dot_general | solution.py:16
  284.2 6.0 %convolution_add_fusion = f32[2,1024,256]{2,1,0:T(8,128)} fusion(f32[2,1024,256]{2,1,0:T(8,128)S(1)} %fusion.31, f32[2,256,1024]{2,1,0:T(8,128)S(1)} %bitcast.146, s32[256]{0:T(256)S(1)} %fusion.88), kind=kOutput, calls=%fused_computation.23 | convolution fusion | flops 1612054528 | bytes 6292480 | tf_op jit(solution)/shard_map/qp,jpc->jqc/dot_general | solution.py:16
  290.3 71.2 %all-to-all-done.2 = f32[2,16,32,1024]{3,2,0,1:T(8,128)} async-done(((f32[2,16,32,1024]{3,2,0,1:T(8,128)}), f32[2,16,32,1024]{3,2,0,1:T(8,128)}, u32[]{:S(2)}, u32[]{:S(2)}) %all-to-all-start.2) | async-done | bytes 4194336 | tf_op jit(solution)/shard_map/all_to_all | solution.py:99
  361.4 2.5 copy.56
  363.9 0.6 fusion.170
  364.8 4.4 fusion.33
  369.4 4.5 fusion.29
  373.9 4.7 convolution_add_fusion.1
  378.7 4.3 convolution_subtract_fusion
  383.0 5.0 multiply_subtract_fusion
  388.1 2.8 fusion.2
  390.9 2.8 fusion
  393.7 2.8 fusion.8
  396.6 3.4 subtract_bitcast_fusion
  399.9 2.2 pad_maximum_fusion.2
  402.1 7.4 %copy.74 = f32[2,2,256,1024]{3,1,0,2:T(2,128)} copy(f32[2,2,256,1024]{2,3,1,0:T(8,128)} %pad_maximum_fusion.2) | data formatting | bytes 8388608 | tf_op jit(solution)/shard_map/stack | solution.py:124
  409.6 96.4 %all_to_all.126 = f32[2,2,256,1024]{3,1,0,2:T(2,128)S(1)} all-to-all(f32[2,2,256,1024]{3,1,0,2:T(2,128)} %copy.74), channel_id=1, replica_groups=mesh['seq'=8,'ch'=4] {'seq'}, dimensions={2} | all-to-all | bytes 8388608 | tf_op jit(solution)/shard_map/all_to_all | solution.py:123
  506.0 2.4 copy.75
  508.4 1.8 fusion.168
  510.2 1.6 copy.76
  511.8 2.4 squeeze.22
  514.3 2.9 fusion.66
  517.2 3.0 copy.77
  520.1 2.7 squeeze.23
  522.8 1.1 fusion.14
  524.0 0.6 copy.78
  524.6 28.7 %all_to_all.127 = f32[8,1,4,8,1024]{4,3,2,1,0:T(8,128)S(1)} all-to-all(f32[8,1,4,8,1024]{4,3,2,1,0:T(8,128)S(1)} %copy.78), channel_id=1, replica_groups=mesh['seq'=8,'ch'=4] {'seq'}, dimensions={0} | all-to-all | bytes 2097152 | tf_op jit(solution)/shard_map/all_to_all | solution.py:131
  553.2 0.6 copy.79
  553.9 16.5 %all_to_all.128 = f32[1,8,4,8,1024]{4,1,3,0,2:T(8,128)S(1)} all-to-all(f32[1,8,4,8,1024]{4,1,3,0,2:T(8,128)S(1)} %copy.79), channel_id=1, replica_groups=mesh['seq'=8,'ch'=4] {'ch'}, dimensions={2} | all-to-all | bytes 2097152 | tf_op jit(solution)/shard_map/all_to_all | solution.py:130
  570.4 0.7 copy.93
  571.1 0.6 copy.91
  571.7 1.1 multiply_convert_fusion
  (36 shorter events, 2.5 us)
Async XLA Ops:
  0.0 5.6 copy-start.7
  0.0 5.6 copy-start.5
  0.0 29.7 %all-to-all-start.3 = ((f32[1,8,1,8,4096]{4,3,2,0,1:T(8,128)}), f32[1,8,1,8,4096]{4,3,2,0,1:T(8,128)S(1)}, u32[]{:S(2)}, u32[]{:S(2)}) async-start(f32[1,8,1,8,4096]{4,3,2,0,1:T(8,128)} %bitcast.167), calls=%async_computation.3 | async-start | bytes 2097152 | tf_op jit(solution)/shard_map/all_to_all | solution.py:43
  29.7 29.6 %all-to-all-start = ((f32[1,8,1,8,4096]{4,3,2,0,1:T(8,128)}), f32[1,8,1,8,4096]{4,3,2,0,1:T(8,128)S(1)}, u32[]{:S(2)}, u32[]{:S(2)}) async-start(f32[1,8,1,8,4096]{4,3,2,0,1:T(8,128)} %fusion.15), calls=%async_computation | async-start | bytes 2097152 | tf_op jit(solution)/shard_map/all_to_all | solution.py:36
  59.3 24.8 %all-to-all-start.4 = ((f32[4,1,65536]{2,1,0:T(1,128)}), f32[4,1,65536]{2,1,0:T(1,128)S(1)}, u32[]{:S(2)}, u32[]{:S(2)}) async-start(f32[4,1,65536]{2,1,0:T(1,128)} %reshape.292), calls=%async_computation.4 | async-start | bytes 2097152 | tf_op jit(solution)/shard_map/all_to_all | solution.py:42
  84.1 39.7 %all-to-all-start.1 = ((f32[4,1,65536]{2,1,0:T(1,128)}), f32[4,1,65536]{2,1,0:T(1,128)}, u32[]{:S(2)}, u32[]{:S(2)}) async-start(f32[4,1,65536]{2,1,0:T(1,128)} %reshape.290), calls=%async_computation.1 | async-start | bytes 2097152 | tf_op jit(solution)/shard_map/all_to_all | solution.py:35
  153.8 1.9 copy-start
  165.6 6.7 %copy-start.2 = (f32[1,16,32,1024]{3,1,2,0:T(8,128)S(1)}, f32[1,16,32,1024]{3,1,2,0:T(8,128)}, u32[]{:S(2)}) copy-start(f32[1,16,32,1024]{3,1,2,0:T(8,128)} %get-tuple-element.19) | copy-start | bytes 6291460
  165.6 98.3 %all-to-all-start.5 = ((f32[2,16,32,1024]{3,2,0,1:T(8,128)}), f32[2,16,32,1024]{3,2,0,1:T(8,128)}, u32[]{:S(2)}, u32[]{:S(2)}) async-start(f32[2,16,32,1024]{3,2,0,1:T(8,128)} %copy.64), calls=%async_computation.5 | async-start | bytes 8388608 | tf_op jit(solution)/shard_map/all_to_all | solution.py:102
  263.9 97.5 %all-to-all-start.2 = ((f32[2,16,32,1024]{3,2,0,1:T(8,128)}), f32[2,16,32,1024]{3,2,0,1:T(8,128)}, u32[]{:S(2)}, u32[]{:S(2)}) async-start(f32[2,16,32,1024]{3,2,0,1:T(8,128)} %copy.55), calls=%async_computation.2 | async-start | bytes 8388608 | tf_op jit(solution)/shard_map/all_to_all | solution.py:99
  373.9 4.7 copy-start.1
  378.7 4.3 copy-start.4
  514.3 2.9 copy-start.3
  570.4 1.3 copy-start.6
  570.4 1.3 copy-start.8
  570.4 1.4 copy-start.9
  570.4 1.4 copy-start.10
where the time goes:
time: 584 us; the launch traced here: 573 us
  waiting for transfers between devices  183 us (31%)
  blocking collectives  142 us (24%)
  local copies, waits for them, and re-layouts  133 us (23%)
  matrix products  66.9 us (11%)
  starting transfers between devices  32.9 us (6%)
  other arithmetic  15.6 us (3%)
    all_to_all x1, blocking collectives, shards(): lax.all_to_all(jnp.stack([turned_real, turned_imag]), 'seq', split_axis=2...  96.4 us
    all_to_all x1, waiting for transfers between devices, shards(): lax.all_to_all(forward_blocks(moved_filter), 'seq', split_axis=1, concat_...  85.2 us
    all_to_all x1, waiting for transfers between devices, shards(): lax.all_to_all(forward_blocks(moved_signal), 'seq', split_axis=1, concat_...  71.2 us
    dot_general x18, matrix products, contract(): jnp.einsum(pattern, weights, operand, precision=highest, preferred_elemen...  66.9 us
    unnamed x27, local copies, waits for them, and re-layouts  54.3 us
    all_to_all x1, blocking collectives, shards(): lax.all_to_all(convolved.reshape(seq_count, 1, group_count, per_peer, col...  28.7 us
    all_to_all x1, waiting for transfers between devices, shards(): lax.all_to_all(filter_taps.reshape(layout), 'seq', split_axis=1, concat_a...  23 us
    all_to_all x1, blocking collectives, shards(): lax.all_to_all(lax.all_to_all(convolved.reshape(seq_count, 1, group_count...  16.5 us
  transfers between devices with their start and end apart: 6, of which 4 were waited for; matrix products, arithmetic and copies ran while one was open for 18% of the time, Pallas kernels for 0%

commit v1 on v0

--- a/solution.py
+++ b/solution.py
@@ -1,8 +1,13 @@
+import functools
 import math
 
 import jax
 import jax.numpy as jnp
+import ml_dtypes
+import numpy as np
 from jax import lax
+from jax.experimental import pallas as pl
+from jax.experimental.pallas import tpu as pltpu
 from jax.sharding import PartitionSpec as P
 
 highest = lax.Precision.HIGHEST
@@ -18,7 +23,7 @@
     )
 
 
-def shards(query_rows, key_rows, value_rows, filter_taps, skip_gain):
+def staged_shards(query_rows, key_rows, value_rows, filter_taps, skip_gain):
     seq_count = lax.axis_size("seq")
     group_count = lax.axis_size("ch")
     position = lax.axis_index("seq")
@@ -145,7 +150,246 @@
     return gated.astype(jnp.bfloat16)
 
 
+MESH = pl.DeviceIdType.MESH
+LANES = 128
+
+
+def split_bf16(values):
+    high = values.astype(ml_dtypes.bfloat16)
+    low = (values - high.astype(np.float64)).astype(ml_dtypes.bfloat16)
+    return high, low
+
+
+def block_transforms(block):
+    order = np.concatenate([np.arange(0, block, 2), np.arange(1, block, 2)])
+    phase = np.pi / block * (order[:, None] + 0.5) * np.arange(block)[None, :]
+    forward = np.concatenate([np.cos(phase), -np.sin(phase)], axis=0)
+    inverse = np.concatenate([np.cos(phase).T, -np.sin(phase).T], axis=1) / block
+    forward_high, forward_low = split_bf16(forward)
+    inverse_high, inverse_low = split_bf16(inverse)
+    return (
+        np.concatenate([forward_high, forward_high, forward_low], axis=1),
+        np.concatenate([inverse_high, inverse_high, inverse_low], axis=1),
+    )
+
+
+def three_parts(values):
+    high = values.astype(jnp.bfloat16)
+    low = (values - high.astype(jnp.float32)).astype(jnp.bfloat16)
+    return jnp.concatenate([high, low, high], axis=0)
+
+
+def conv_kernel(
+    seq_count,
+    group_count,
+    key_ref,
+    value_ref,
+    taps_ref,
+    query_ref,
+    gain_ref,
+    forward_hbm,
+    inverse_hbm,
+    out_ref,
+    signal,
+    signal_in,
+    taps_in,
+    conv,
+    conv_in,
+    spectra,
+    windows,
+    product,
+    forward_mat,
+    inverse_mat,
+    send_sem,
+    signal_sem,
+    taps_sem,
+    conv_sem,
+    const_sem,
+):
+    position = lax.axis_index("seq")
+    group = lax.axis_index("ch")
+    peers = seq_count * group_count
+    me = position * group_count + group
+    rows = key_ref.shape[0]
+    block = rows * group_count
+    half = block // 2
+
+    def peer_of(step):
+        there = lax.rem(position + step // group_count, seq_count)
+        across = lax.rem(group + lax.rem(step, group_count), group_count)
+        return there, across
+
+    barrier = pltpu.get_barrier_semaphore()
+
+    def greet(step, carry):
+        pl.semaphore_signal(barrier, inc=1, device_id=peer_of(step), device_id_type=MESH)
+        return carry
+
+    lax.fori_loop(1, peers, greet, 0)
+    load_forward = pltpu.make_async_copy(forward_hbm, forward_mat, const_sem.at[0])
+    load_inverse = pltpu.make_async_copy(inverse_hbm, inverse_mat, const_sem.at[1])
+    load_forward.start()
+    load_inverse.start()
+    signal[...] = key_ref[...].astype(jnp.float32) * value_ref[...].astype(jnp.float32)
+    pl.semaphore_wait(barrier, peers - 1)
+
+    my_rows = pl.ds(pl.multiple_of(me * rows, rows), rows)
+    my_lanes = pl.ds(pl.multiple_of(me * LANES, LANES), LANES)
+
+    def send(step, carry):
+        there, across = peer_of(step)
+        peer = there * group_count + across
+        lanes = pl.ds(pl.multiple_of(peer * LANES, LANES), LANES)
+        pltpu.make_async_remote_copy(
+            src_ref=signal.at[:, lanes],
+            dst_ref=signal_in.at[my_rows, :],
+            send_sem=send_sem.at[0],
+            recv_sem=signal_sem.at[position],
+            device_id=(there, across),
+            device_id_type=MESH,
+        ).start()
+        pltpu.make_async_remote_copy(
+            src_ref=taps_ref.at[:, lanes],
+            dst_ref=taps_in.at[my_rows, :],
+            send_sem=send_sem.at[1],
+            recv_sem=taps_sem.at[position],
+            device_id=(there, across),
+            device_id_type=MESH,
+        ).start()
+        return carry
+
+    lax.fori_loop(1, peers, send, 0)
+    pltpu.make_async_copy(
+        signal.at[:, my_lanes], signal_in.at[my_rows, :], signal_sem.at[position]
+    ).start()
+    pltpu.make_async_copy(
+        taps_ref.at[:, my_lanes], taps_in.at[my_rows, :], taps_sem.at[position]
+    ).start()
+    load_forward.wait()
+    load_inverse.wait()
+
+    for d in range(seq_count):
+        here = pl.ds(d * block, block)
+        pltpu.make_async_copy(signal_in.at[here, :], signal_in.at[here, :], signal_sem.at[d]).wait()
+        pltpu.make_async_copy(taps_in.at[here, :], taps_in.at[here, :], taps_sem.at[d]).wait()
+        both = jnp.concatenate([signal_in[here, :], taps_in[here, :]], axis=1)
+        spectrum = jnp.dot(
+            forward_mat[...], three_parts(both), preferred_element_type=jnp.float32
+        )
+        spectra[d] = spectrum[:, :LANES]
+        tap_spectrum = spectrum[:, LANES:]
+        if d == 0:
+            windows[0] = tap_spectrum
+        else:
+            windows[d] += tap_spectrum
+        if d + 1 < seq_count:
+            windows[d + 1, 0:half] = -tap_spectrum[block : block + half]
+            windows[d + 1, half:block] = tap_spectrum[block + half :]
+            windows[d + 1, block : block + half] = tap_spectrum[0:half]
+            windows[d + 1, block + half :] = -tap_spectrum[half:block]
+
+        def multiply(chunk, carry):
+            real = pl.ds(pl.multiple_of(chunk * 32, 32), 32)
+            imag = pl.ds(pl.multiple_of(block + chunk * 32, 32), 32)
+            total_real = jnp.zeros((32, LANES), jnp.float32)
+            total_imag = jnp.zeros((32, LANES), jnp.float32)
+            for j in range(d + 1):
+                s_real = spectra[j, real, :]
+                s_imag = spectra[j, imag, :]
+                f_real = windows[d - j, real, :]
+                f_imag = windows[d - j, imag, :]
+                total_real += s_real * f_real - s_imag * f_imag
+                total_imag += s_real * f_imag + s_imag * f_real
+            product[real, :] = total_real
+            product[imag, :] = total_imag
+            return carry
+
+        lax.fori_loop(0, block // 32, multiply, 0)
+        conv[here, :] = jnp.dot(
+            inverse_mat[...], three_parts(product[...]), preferred_element_type=jnp.float32
+        )
+        for c in range(group_count):
+            owner = d * group_count + c
+            piece = conv.at[pl.ds(owner * rows, rows), :]
+
+            @pl.when(owner != me)
+            def _():
+                pltpu.make_async_remote_copy(
+                    src_ref=piece,
+                    dst_ref=conv_in.at[:, my_lanes],
+                    send_sem=send_sem.at[2],
+                    recv_sem=conv_sem.at[position],
+                    device_id=(d, c),
+                    device_id_type=MESH,
+                ).start()
+
+            @pl.when(owner == me)
+            def _():
+                pltpu.make_async_copy(piece, conv_in.at[:, my_lanes], conv_sem.at[position]).start()
+
+    width = group_count * LANES
+    for d in range(seq_count):
+        lanes = pl.ds(d * width, width)
+        pltpu.make_async_copy(conv_in.at[:, lanes], conv_in.at[:, lanes], conv_sem.at[d]).wait()
+        skipped = gain_ref[0:1, lanes] * signal[:, lanes]
+        out_ref[:, lanes] = (
+            query_ref[:, lanes].astype(jnp.float32) * (conv_in[:, lanes] + skipped)
+        ).astype(jnp.bfloat16)
+
+    sent = pl.ds(0, (peers - 1) * rows)
+    for which in range(3):
+        pltpu.make_async_copy(
+            signal_in.at[sent, :], signal_in.at[sent, :], send_sem.at[which]
+        ).wait()
+
+
+def fused_shards(query_rows, key_rows, value_rows, filter_taps, skip_gain):
+    seq_count = lax.axis_size("seq")
+    group_count = lax.axis_size("ch")
+    rows, full_width = key_rows.shape
+    block = rows * group_count
+    tokens = block * seq_count
+    forward, inverse = block_transforms(block)
+    in_vmem = pl.BlockSpec(memory_space=pltpu.VMEM)
+    in_any = pl.BlockSpec(memory_space=pl.ANY)
+    return pl.pallas_call(
+        functools.partial(conv_kernel, seq_count, group_count),
+        out_shape=jax.ShapeDtypeStruct((rows, full_width), jnp.bfloat16),
+        in_specs=[in_vmem] * 5 + [in_any] * 2,
+        out_specs=in_vmem,
+        scratch_shapes=[
+            pltpu.VMEM((rows, full_width), jnp.float32),
+            pltpu.VMEM((tokens, LANES), jnp.float32),
+            pltpu.VMEM((tokens, LANES), jnp.float32),
+            pltpu.VMEM((tokens, LANES), jnp.float32),
+            pltpu.VMEM((rows, full_width), jnp.float32),
+            pltpu.VMEM((seq_count, 2 * block, LANES), jnp.float32),
+            pltpu.VMEM((seq_count, 2 * block, LANES), jnp.float32),
+            pltpu.VMEM((2 * block, LANES), jnp.float32),
+            pltpu.VMEM(forward.shape, jnp.bfloat16),
+            pltpu.VMEM(inverse.shape, jnp.bfloat16),
+            pltpu.SemaphoreType.DMA((3,)),
+            pltpu.SemaphoreType.DMA((seq_count,)),
+            pltpu.SemaphoreType.DMA((seq_count,)),
+            pltpu.SemaphoreType.DMA((seq_count,)),
+            pltpu.SemaphoreType.DMA((2,)),
+        ],
+        compiler_params=pltpu.CompilerParams(
+            collective_id=0, has_side_effects=True, vmem_limit_bytes=48 * 1024 * 1024
+        ),
+    )(
+        key_rows,
+        value_rows,
+        filter_taps,
+        query_rows,
+        skip_gain.reshape(1, full_width),
+        jnp.asarray(forward),
+        jnp.asarray(inverse),
+    )
+
+
 def solution(mesh):
+    device_count = mesh.shape["seq"] * mesh.shape["ch"]
     in_specs = (
         P(("seq", "ch"), None),
         P(("seq", "ch"), None),
@@ -154,4 +398,14 @@
         P(),
     )
     out_specs = P(("seq", "ch"), None)
-    return jax.shard_map(shards, mesh=mesh, in_specs=in_specs, out_specs=out_specs, check_vma=False)
+
+    def program(query_rows, key_rows, value_rows, filter_taps, skip_gain):
+        tokens, channels = key_rows.shape
+        one_tile_each = channels == LANES * device_count
+        tiled_rows = tokens % (16 * device_count) == 0
+        body = fused_shards if one_tile_each and tiled_rows else staged_shards
+        return jax.shard_map(
+            body, mesh=mesh, in_specs=in_specs, out_specs=out_specs, check_vma=False
+        )(query_rows, key_rows, value_rows, filter_taps, skip_gain)
+
+    return program

time: 584 us -> 88.1 us (0.15); the launches traced: 573 us -> 87.7 us
  waiting for transfers between devices: 183 us -> 0 us
  blocking collectives: 142 us -> 0 us
  local copies, waits for them, and re-layouts: 133 us -> 8.13 us
  Pallas kernels: 0 us -> 79.5 us
  matrix products: 66.9 us -> 0 us
  starting transfers between devices: 32.9 us -> 0 us
  other arithmetic: 15.6 us -> 0 us
    all_to_all x6 -> x0, waiting for transfers between devices: 183 us -> none  [the longest x1 85.2 us: shards(): lax.all_to_all(forward_blocks(moved_filter), 'seq', split_axis=1, concat_...]
    all_to_all x3 -> x0, blocking collectives: 142 us -> none  [the longest x1 96.4 us: shards(): lax.all_to_all(jnp.stack([turned_real, turned_imag]), 'seq', split_axis=2...]
    pallas_call x0 -> x1, Pallas kernels: none -> 79.5 us  [fused_shards(): pl.pallas_call(functools.partial(conv_kernel, seq_count, group_count), ou...]
    dot_general x18 -> x0, matrix products: 66.9 us -> none  [contract(): jnp.einsum(pattern, weights, operand, precision=highest, preferred_elemen...]
    all_to_all x12 -> x0, local copies, waits for them, and re-layouts: 47.8 us -> none  [the longest x3 11.1 us: shards(): lax.all_to_all(lax.all_to_all(filter_taps.reshape(layout), 'seq', split_a...]
    unnamed x27 -> x15, local copies, waits for them, and re-layouts: 54.3 us -> 8.13 us
    all_to_all x6 -> x0, starting transfers between devices: 32.9 us -> none  [the longest x1 6.69 us: shards(): lax.all_to_all(forward_blocks(moved_filter), 'seq', split_axis=1, concat_...]
    another operation x3 -> x0, local copies, waits for them, and re-layouts: 16.3 us -> none  [the longest x2 8.86 us: forward_blocks(): jnp.stack([out_real * twist_cos - out_imag * twist_sin, out_real * twist_...]
  transfers between devices with their start and end apart: 6 -> 0, of which waited for: 4 -> 0; matrix products, arithmetic and copies ran while one was open for 18% -> 0% of each run, Pallas kernels for 0% -> 0%
where the time goes in v1:
time: 88.1 us; the launch traced here: 87.7 us
  Pallas kernels  79.5 us (90%)
  local copies, waits for them, and re-layouts  8.13 us (9%)
    pallas_call x1, Pallas kernels, fused_shards(): pl.pallas_call(functools.partial(conv_kernel, seq_count, group_count), ou...  79.5 us
    unnamed x15, local copies, waits for them, and re-layouts  8.13 us

profile of v1, /device:TPU:31, one launch (start us, length us, event | category | flops | bytes accessed | tf_op | source)
XLA Modules:
  0.0 87.7 jit_solution(17383012630505316661)
XLA Ops:
  0.0 0.0 copy-start
  0.0 1.2 %copy-done = f32[64,4096]{1,0:T(8,128)S(1)} copy-done((f32[64,4096]{1,0:T(8,128)S(1)}, f32[64,4096]{1,0:T(8,128)}, u32[]{:S(2)}) %copy-start) | copy-done | bytes 1048600
  1.2 0.0 copy-start.1
  1.2 1.1 %copy-done.1 = bf16[256,1536]{1,0:T(8,128)(2,1)S(1)} copy-done((bf16[256,1536]{1,0:T(8,128)(2,1)S(1)}, bf16[256,1536]{1,0:T(8,128)(2,1)}, u32[]{:S(2)}) %copy-start.1) | copy-done | bytes 786456
  2.4 0.0 copy-start.2
  2.4 1.1 %copy-done.2 = bf16[512,768]{1,0:T(8,128)(2,1)S(1)} copy-done((bf16[512,768]{1,0:T(8,128)(2,1)S(1)}, bf16[512,768]{1,0:T(8,128)(2,1)}, u32[]{:S(2)}) %copy-start.2) | copy-done | bytes 786456
  3.5 0.0 copy-start.3
  3.5 1.0 %copy-done.3 = bf16[64,4096]{1,0:T(8,128)(2,1)S(1)} copy-done((bf16[64,4096]{1,0:T(8,128)(2,1)S(1)}, bf16[64,4096]{1,0:T(8,128)(2,1)}, u32[]{:S(2)}) %copy-start.3) | copy-done | bytes 524312
  4.5 0.0 copy-start.4
  4.5 1.0 %copy-done.4 = bf16[64,4096]{1,0:T(8,128)(2,1)S(1)} copy-done((bf16[64,4096]{1,0:T(8,128)(2,1)S(1)}, bf16[64,4096]{1,0:T(8,128)(2,1)}, u32[]{:S(2)}) %copy-start.4) | copy-done | bytes 524312
  5.6 0.0 copy-start.5
  5.6 1.0 %copy-done.5 = bf16[64,4096]{1,0:T(8,128)(2,1)S(1)} copy-done((bf16[64,4096]{1,0:T(8,128)(2,1)S(1)}, bf16[64,4096]{1,0:T(8,128)(2,1)}, u32[]{:S(2)}) %copy-start.5) | copy-done | bytes 524312
  6.6 0.0 copy-start.6
  6.6 0.7 copy-done.6
  7.3 79.5 %shard_map.73 = bf16[64,4096]{1,0:T(8,128)(2,1)S(1)} custom-call(bf16[64,4096]{1,0:T(8,128)(2,1)S(1)} %copy-done.3, bf16[64,4096]{1,0:T(8,128)(2,1)S(1)} %copy-done.4, f32[64,4096]{1,0:T(8,128)S(1)} %copy-done, bf16[64,4096]{1,0:T(8,128)(2,1)S(1)} %copy-done.5, f32[1,4096]{1,0:T(1,128)S(1)} %bitcast.1, bf16[512,768]{1,0:T(8,128)(2,1)S(1)} %copy-done.2, ...), custom_call_target="tpu_custom_call" | custom-call | tf_op jit(solution)/shard_map/pallas_call | solution.py:355
  86.9 0.8 copy.9
Async XLA Ops:
  0.0 1.2 %copy-start = (f32[64,4096]{1,0:T(8,128)S(1)}, f32[64,4096]{1,0:T(8,128)}, u32[]{:S(2)}) copy-start(f32[64,4096]{1,0:T(8,128)} %taps_ref.1) | copy-start | bytes 3145732
  1.2 1.1 %copy-start.1 = (bf16[256,1536]{1,0:T(8,128)(2,1)S(1)}, bf16[256,1536]{1,0:T(8,128)(2,1)}, u32[]{:S(2)}) copy-start(bf16[256,1536]{1,0:T(8,128)(2,1)} %constant.5.clone.inverse_hbm) | copy-start | bytes 2359300
  2.4 1.1 %copy-start.2 = (bf16[512,768]{1,0:T(8,128)(2,1)S(1)}, bf16[512,768]{1,0:T(8,128)(2,1)}, u32[]{:S(2)}) copy-start(bf16[512,768]{1,0:T(8,128)(2,1)} %constant.4.clone.forward_hbm) | copy-start | bytes 2359300
  3.5 1.0 %copy-start.3 = (bf16[64,4096]{1,0:T(8,128)(2,1)S(1)}, bf16[64,4096]{1,0:T(8,128)(2,1)}, u32[]{:S(2)}) copy-start(bf16[64,4096]{1,0:T(8,128)(2,1)} %key_ref.1) | copy-start | bytes 1572868
  4.5 1.0 %copy-start.4 = (bf16[64,4096]{1,0:T(8,128)(2,1)S(1)}, bf16[64,4096]{1,0:T(8,128)(2,1)}, u32[]{:S(2)}) copy-start(bf16[64,4096]{1,0:T(8,128)(2,1)} %value_ref.1) | copy-start | bytes 1572868
  5.6 1.0 %copy-start.5 = (bf16[64,4096]{1,0:T(8,128)(2,1)S(1)}, bf16[64,4096]{1,0:T(8,128)(2,1)}, u32[]{:S(2)}) copy-start(bf16[64,4096]{1,0:T(8,128)(2,1)} %query_ref.1) | copy-start | bytes 1572868
  6.6 0.7 copy-start.6

commit v2 on v1

--- a/solution.py
+++ b/solution.py
@@ -182,14 +182,18 @@
 def conv_kernel(
     seq_count,
     group_count,
-    key_ref,
-    value_ref,
-    taps_ref,
-    query_ref,
-    gain_ref,
+    key_hbm,
+    value_hbm,
+    taps_hbm,
+    query_hbm,
+    gain_hbm,
     forward_hbm,
     inverse_hbm,
     out_ref,
+    key_ref,
+    value_ref,
+    query_ref,
+    gain_ref,
     signal,
     signal_in,
     taps_in,
@@ -204,7 +208,7 @@
     signal_sem,
     taps_sem,
     conv_sem,
-    const_sem,
+    load_sem,
 ):
     position = lax.axis_index("seq")
     group = lax.axis_index("ch")
@@ -213,63 +217,88 @@
     rows = key_ref.shape[0]
     block = rows * group_count
     half = block // 2
-
-    def peer_of(step):
+    half_seq = seq_count // 2
+    upper = position // half_seq
+    turns = 2 if group_count % 2 == 0 else 1
+    per_turn = group_count // turns
+
+    loads = [
+        pltpu.make_async_copy(source, target, load_sem.at[n])
+        for n, (source, target) in enumerate(
+            [
+                (key_hbm, key_ref),
+                (value_hbm, value_ref),
+                (forward_hbm, forward_mat),
+                (inverse_hbm, inverse_mat),
+                (query_hbm, query_ref),
+                (gain_hbm, gain_ref),
+            ]
+        )
+    ]
+    loads[0].start()
+    loads[1].start()
+    barrier = pltpu.get_barrier_semaphore()
+
+    def greet(step, carry):
         there = lax.rem(position + step // group_count, seq_count)
         across = lax.rem(group + lax.rem(step, group_count), group_count)
-        return there, across
-
-    barrier = pltpu.get_barrier_semaphore()
-
-    def greet(step, carry):
-        pl.semaphore_signal(barrier, inc=1, device_id=peer_of(step), device_id_type=MESH)
+        pl.semaphore_signal(barrier, inc=1, device_id=(there, across), device_id_type=MESH)
         return carry
 
     lax.fori_loop(1, peers, greet, 0)
-    load_forward = pltpu.make_async_copy(forward_hbm, forward_mat, const_sem.at[0])
-    load_inverse = pltpu.make_async_copy(inverse_hbm, inverse_mat, const_sem.at[1])
-    load_forward.start()
-    load_inverse.start()
+    loads[0].wait()
+    loads[1].wait()
     signal[...] = key_ref[...].astype(jnp.float32) * value_ref[...].astype(jnp.float32)
+    for load in loads[2:]:
+        load.start()
     pl.semaphore_wait(barrier, peers - 1)
 
     my_rows = pl.ds(pl.multiple_of(me * rows, rows), rows)
     my_lanes = pl.ds(pl.multiple_of(me * LANES, LANES), LANES)
 
     def send(step, carry):
-        there, across = peer_of(step)
+        turn = step // (seq_count * per_turn)
+        inner = lax.rem(step, seq_count * per_turn)
+        hop = inner // per_turn
+        across = turns * lax.rem(group // turns + lax.rem(inner, per_turn), per_turn) + turn
+        side = lax.rem(upper + 1 + lax.rem(hop, 2), 2)
+        there = side * half_seq + lax.rem(position + hop // 2, half_seq)
         peer = there * group_count + across
         lanes = pl.ds(pl.multiple_of(peer * LANES, LANES), LANES)
-        pltpu.make_async_remote_copy(
-            src_ref=signal.at[:, lanes],
-            dst_ref=signal_in.at[my_rows, :],
-            send_sem=send_sem.at[0],
-            recv_sem=signal_sem.at[position],
-            device_id=(there, across),
-            device_id_type=MESH,
-        ).start()
-        pltpu.make_async_remote_copy(
-            src_ref=taps_ref.at[:, lanes],
-            dst_ref=taps_in.at[my_rows, :],
-            send_sem=send_sem.at[1],
-            recv_sem=taps_sem.at[position],
-            device_id=(there, across),
-            device_id_type=MESH,
-        ).start()
+
+        @pl.when(peer != me)
+        def _():
+            pltpu.make_async_remote_copy(
+                src_ref=taps_hbm.at[:, lanes],
+                dst_ref=taps_in.at[my_rows, :],
+                send_sem=send_sem.at[1],
+                recv_sem=taps_sem.at[position],
+                device_id=(there, across),
+                device_id_type=MESH,
+            ).start()
+            pltpu.make_async_remote_copy(
+                src_ref=signal.at[:, lanes],
+                dst_ref=signal_in.at[my_rows, :],
+                send_sem=send_sem.at[0],
+                recv_sem=signal_sem.at[position],
+                device_id=(there, across),
+                device_id_type=MESH,
+            ).start()
+
         return carry
 
-    lax.fori_loop(1, peers, send, 0)
     pltpu.make_async_copy(
         signal.at[:, my_lanes], signal_in.at[my_rows, :], signal_sem.at[position]
     ).start()
     pltpu.make_async_copy(
-        taps_ref.at[:, my_lanes], taps_in.at[my_rows, :], taps_sem.at[position]
+        taps_hbm.at[:, my_lanes], taps_in.at[my_rows, :], taps_sem.at[position]
     ).start()
-    load_forward.wait()
-    load_inverse.wait()
-
-    for d in range(seq_count):
-        here = pl.ds(d * block, block)
+    lax.fori_loop(0, peers, send, 0)
+    for load in loads[2:]:
+        load.wait()
+
+    def transform(d, carry):
+        here = pl.ds(pl.multiple_of(d * block, block), block)
         pltpu.make_async_copy(signal_in.at[here, :], signal_in.at[here, :], signal_sem.at[d]).wait()
         pltpu.make_async_copy(taps_in.at[here, :], taps_in.at[here, :], taps_sem.at[d]).wait()
         both = jnp.concatenate([signal_in[here, :], taps_in[here, :]], axis=1)
@@ -278,39 +307,39 @@
         )
         spectra[d] = spectrum[:, :LANES]
         tap_spectrum = spectrum[:, LANES:]
-        if d == 0:
-            windows[0] = tap_spectrum
-        else:
-            windows[d] += tap_spectrum
-        if d + 1 < seq_count:
-            windows[d + 1, 0:half] = -tap_spectrum[block : block + half]
-            windows[d + 1, half:block] = tap_spectrum[block + half :]
-            windows[d + 1, block : block + half] = tap_spectrum[0:half]
-            windows[d + 1, block + half :] = -tap_spectrum[half:block]
-
-        def multiply(chunk, carry):
-            real = pl.ds(pl.multiple_of(chunk * 32, 32), 32)
-            imag = pl.ds(pl.multiple_of(block + chunk * 32, 32), 32)
-            total_real = jnp.zeros((32, LANES), jnp.float32)
-            total_imag = jnp.zeros((32, LANES), jnp.float32)
-            for j in range(d + 1):
+        windows[d] += tap_spectrum
+        windows[d + 1, 0:half] = -tap_spectrum[block : block + half]
+        windows[d + 1, half:block] = tap_spectrum[block + half :]
+        windows[d + 1, block : block + half] = tap_spectrum[0:half]
+        windows[d + 1, block + half :] = -tap_spectrum[half:block]
+        return carry
+
+    chunk_rows = 64
+
+    def output(d, carry):
+        for chunk in range(block // chunk_rows):
+            real = pl.ds(chunk * chunk_rows, chunk_rows)
+            imag = pl.ds(block + chunk * chunk_rows, chunk_rows)
+
+            def pair(j, totals):
                 s_real = spectra[j, real, :]
                 s_imag = spectra[j, imag, :]
                 f_real = windows[d - j, real, :]
                 f_imag = windows[d - j, imag, :]
-                total_real += s_real * f_real - s_imag * f_imag
-                total_imag += s_real * f_imag + s_imag * f_real
-            product[real, :] = total_real
-            product[imag, :] = total_imag
-            return carry
-
-        lax.fori_loop(0, block // 32, multiply, 0)
+                return (
+                    totals[0] + (s_real * f_real - s_imag * f_imag),
+                    totals[1] + (s_real * f_imag + s_imag * f_real),
+                )
+
+            zero = jnp.zeros((chunk_rows, LANES), jnp.float32)
+            product[real, :], product[imag, :] = lax.fori_loop(0, d + 1, pair, (zero, zero))
+        here = pl.ds(pl.multiple_of(d * block, block), block)
         conv[here, :] = jnp.dot(
             inverse_mat[...], three_parts(product[...]), preferred_element_type=jnp.float32
         )
         for c in range(group_count):
             owner = d * group_count + c
-            piece = conv.at[pl.ds(owner * rows, rows), :]
+            piece = conv.at[pl.ds(pl.multiple_of(owner * rows, rows), rows), :]
 
             @pl.when(owner != me)
             def _():
@@ -327,14 +356,27 @@
             def _():
                 pltpu.make_async_copy(piece, conv_in.at[:, my_lanes], conv_sem.at[position]).start()
 
+        return carry
+
+    windows[0] = jnp.zeros((2 * block, LANES), jnp.float32)
+    lax.fori_loop(0, half_seq, transform, 0)
+    lax.fori_loop(0, half_seq * upper, output, 0)
+    lax.fori_loop(half_seq, seq_count, transform, 0)
+    lax.fori_loop(half_seq, seq_count, output, 0)
+    lax.fori_loop(0, half_seq * (1 - upper), output, 0)
+
     width = group_count * LANES
-    for d in range(seq_count):
-        lanes = pl.ds(d * width, width)
+
+    def finish(d, carry):
+        lanes = pl.ds(pl.multiple_of(d * width, width), width)
         pltpu.make_async_copy(conv_in.at[:, lanes], conv_in.at[:, lanes], conv_sem.at[d]).wait()
         skipped = gain_ref[0:1, lanes] * signal[:, lanes]
         out_ref[:, lanes] = (
             query_ref[:, lanes].astype(jnp.float32) * (conv_in[:, lanes] + skipped)
         ).astype(jnp.bfloat16)
+        return carry
+
+    lax.fori_loop(0, seq_count, finish, 0)
 
     sent = pl.ds(0, (peers - 1) * rows)
     for which in range(3):
@@ -351,20 +393,24 @@
     tokens = block * seq_count
     forward, inverse = block_transforms(block)
     in_vmem = pl.BlockSpec(memory_space=pltpu.VMEM)
-    in_any = pl.BlockSpec(memory_space=pl.ANY)
+    in_hbm = pl.BlockSpec(memory_space=pltpu.HBM)
     return pl.pallas_call(
         functools.partial(conv_kernel, seq_count, group_count),
         out_shape=jax.ShapeDtypeStruct((rows, full_width), jnp.bfloat16),
-        in_specs=[in_vmem] * 5 + [in_any] * 2,
+        in_specs=[in_hbm] * 7,
         out_specs=in_vmem,
         scratch_shapes=[
+            pltpu.VMEM((rows, full_width), jnp.bfloat16),
+            pltpu.VMEM((rows, full_width), jnp.bfloat16),
+            pltpu.VMEM((rows, full_width), jnp.bfloat16),
+            pltpu.VMEM((1, full_width), jnp.float32),
             pltpu.VMEM((rows, full_width), jnp.float32),
             pltpu.VMEM((tokens, LANES), jnp.float32),
             pltpu.VMEM((tokens, LANES), jnp.float32),
             pltpu.VMEM((tokens, LANES), jnp.float32),
             pltpu.VMEM((rows, full_width), jnp.float32),
             pltpu.VMEM((seq_count, 2 * block, LANES), jnp.float32),
-            pltpu.VMEM((seq_count, 2 * block, LANES), jnp.float32),
+            pltpu.VMEM((seq_count + 1, 2 * block, LANES), jnp.float32),
             pltpu.VMEM((2 * block, LANES), jnp.float32),
             pltpu.VMEM(forward.shape, jnp.bfloat16),
             pltpu.VMEM(inverse.shape, jnp.bfloat16),
@@ -372,10 +418,10 @@
             pltpu.SemaphoreType.DMA((seq_count,)),
             pltpu.SemaphoreType.DMA((seq_count,)),
             pltpu.SemaphoreType.DMA((seq_count,)),
-            pltpu.SemaphoreType.DMA((2,)),
+            pltpu.SemaphoreType.DMA((6,)),
         ],
         compiler_params=pltpu.CompilerParams(
-            collective_id=0, has_side_effects=True, vmem_limit_bytes=48 * 1024 * 1024
+            collective_id=0, has_side_effects=True, vmem_limit_bytes=127 * 512 * 1024
         ),
     )(
         key_rows,
@@ -401,7 +447,7 @@
 
     def program(query_rows, key_rows, value_rows, filter_taps, skip_gain):
         tokens, channels = key_rows.shape
-        one_tile_each = channels == LANES * device_count
+        one_tile_each = channels == LANES * device_count and mesh.shape["seq"] % 2 == 0
         tiled_rows = tokens % (16 * device_count) == 0
         body = fused_shards if one_tile_each and tiled_rows else staged_shards
         return jax.shard_map(

time: 88.1 us -> 77.5 us (0.88)
  local copies, waits for them, and re-layouts: 8.13 us -> 1.87 us
  Pallas kernels: 79.5 us -> 75.3 us
    unnamed x15 -> x1, local copies, waits for them, and re-layouts: 8.13 us -> 1.87 us
    pallas_call x1, Pallas kernels: 79.5 us -> 75.3 us  [fused_shards(): pl.pallas_call(functools.partial(conv_kernel, seq_count, group_count), ou...]
where the time goes in v2:
time: 77.5 us; the launch traced here: 77.1 us
  Pallas kernels  75.3 us (97%)
  local copies, waits for them, and re-layouts  1.87 us (2%)
    pallas_call x1, Pallas kernels, fused_shards(): pl.pallas_call(functools.partial(conv_kernel, seq_count, group_count), ou...  75.3 us
    unnamed x1, local copies, waits for them, and re-layouts  1.87 us

profile of v2, /device:TPU:31, one launch (start us, length us, event | category | flops | bytes accessed | tf_op | source)
XLA Modules:
  0.0 77.1 jit_solution(15364538487520527255)
XLA Ops:
  0.0 75.3 %shard_map.73 = bf16[64,4096]{1,0:T(8,128)(2,1)} custom-call(bf16[64,4096]{1,0:T(8,128)(2,1)} %key_hbm.1, bf16[64,4096]{1,0:T(8,128)(2,1)} %value_hbm.1, f32[64,4096]{1,0:T(8,128)} %taps_hbm.1, bf16[64,4096]{1,0:T(8,128)(2,1)} %query_hbm.1, f32[1,4096]{1,0:T(1,128)} %bitcast.1, bf16[512,768]{1,0:T(8,128)(2,1)} %constant.4.clone.forward_hbm, ...), custom_call_target="tpu_custom_call" | custom-call | tf_op jit(solution)/shard_map/pallas_call | solution.py:397
  75.3 1.9 %copy.9 = bf16[64,4096]{1,0:T(8,128)(2,1)} copy(bf16[64,4096]{1,0:T(8,128)(2,1)} %shard_map.73) | data formatting | bytes 1048576

commit v3 on v2

--- a/solution.py
+++ b/solution.py
@@ -189,6 +189,7 @@
     gain_hbm,
     forward_hbm,
     inverse_hbm,
+    out_hbm,
     out_ref,
     key_ref,
     value_ref,
@@ -209,6 +210,7 @@
     taps_sem,
     conv_sem,
     load_sem,
+    store_sem,
 ):
     position = lax.axis_index("seq")
     group = lax.axis_index("ch")
@@ -362,18 +364,24 @@
     lax.fori_loop(0, half_seq, transform, 0)
     lax.fori_loop(0, half_seq * upper, output, 0)
     lax.fori_loop(half_seq, seq_count, transform, 0)
-    lax.fori_loop(half_seq, seq_count, output, 0)
-    lax.fori_loop(0, half_seq * (1 - upper), output, 0)
+    lax.fori_loop(half_seq, seq_count * upper, output, 0)
+
+    def alternate(i, carry):
+        return output(half_seq * lax.rem(i + 1, 2) + i // 2, carry)
+
+    lax.fori_loop(0, seq_count * (1 - upper), alternate, 0)
 
     width = group_count * LANES
 
-    def finish(d, carry):
+    def finish(step, carry):
+        d = lax.rem(step + half_seq * (1 - upper), seq_count)
         lanes = pl.ds(pl.multiple_of(d * width, width), width)
         pltpu.make_async_copy(conv_in.at[:, lanes], conv_in.at[:, lanes], conv_sem.at[d]).wait()
         skipped = gain_ref[0:1, lanes] * signal[:, lanes]
         out_ref[:, lanes] = (
             query_ref[:, lanes].astype(jnp.float32) * (conv_in[:, lanes] + skipped)
         ).astype(jnp.bfloat16)
+        pltpu.make_async_copy(out_ref.at[:, lanes], out_hbm.at[:, lanes], store_sem.at[d]).start()
         return carry
 
     lax.fori_loop(0, seq_count, finish, 0)
@@ -383,6 +391,9 @@
         pltpu.make_async_copy(
             signal_in.at[sent, :], signal_in.at[sent, :], send_sem.at[which]
         ).wait()
+    for d in range(seq_count):
+        lanes = pl.ds(d * width, width)
+        pltpu.make_async_copy(out_ref.at[:, lanes], out_hbm.at[:, lanes], store_sem.at[d]).wait()
 
 
 def fused_shards(query_rows, key_rows, value_rows, filter_taps, skip_gain):
@@ -392,14 +403,14 @@
     block = rows * group_count
     tokens = block * seq_count
     forward, inverse = block_transforms(block)
-    in_vmem = pl.BlockSpec(memory_space=pltpu.VMEM)
     in_hbm = pl.BlockSpec(memory_space=pltpu.HBM)
     return pl.pallas_call(
         functools.partial(conv_kernel, seq_count, group_count),
         out_shape=jax.ShapeDtypeStruct((rows, full_width), jnp.bfloat16),
         in_specs=[in_hbm] * 7,
-        out_specs=in_vmem,
+        out_specs=in_hbm,
         scratch_shapes=[
+            pltpu.VMEM((rows, full_width), jnp.bfloat16),
             pltpu.VMEM((rows, full_width), jnp.bfloat16),
             pltpu.VMEM((rows, full_width), jnp.bfloat16),
             pltpu.VMEM((rows, full_width), jnp.bfloat16),
@@ -419,6 +430,7 @@
             pltpu.SemaphoreType.DMA((seq_count,)),
             pltpu.SemaphoreType.DMA((seq_count,)),
             pltpu.SemaphoreType.DMA((6,)),
+            pltpu.SemaphoreType.DMA((seq_count,)),
         ],
         compiler_params=pltpu.CompilerParams(
             collective_id=0, has_side_effects=True, vmem_limit_bytes=127 * 512 * 1024

time: 77.5 us -> 77.4 us (level)
  no operation moved by 1% of the time
where the time goes in v3:
time: 77.4 us; the launch traced here: 77 us
  Pallas kernels  75.1 us (97%)
  local copies, waits for them, and re-layouts  1.87 us (2%)
    pallas_call x1, Pallas kernels, fused_shards(): pl.pallas_call(functools.partial(conv_kernel, seq_count, group_count), ou...  75.1 us
    unnamed x1, local copies, waits for them, and re-layouts  1.87 us

profile of v3, /device:TPU:31, one launch (start us, length us, event | category | flops | bytes accessed | tf_op | source)
XLA Modules:
  0.0 77.0 jit_solution(17688047878963276088)
XLA Ops:
  0.0 75.1 %shard_map.73 = bf16[64,4096]{1,0:T(8,128)(2,1)} custom-call(bf16[64,4096]{1,0:T(8,128)(2,1)} %key_hbm.1, bf16[64,4096]{1,0:T(8,128)(2,1)} %value_hbm.1, f32[64,4096]{1,0:T(8,128)} %taps_hbm.1, bf16[64,4096]{1,0:T(8,128)(2,1)} %query_hbm.1, f32[1,4096]{1,0:T(1,128)} %bitcast.1, bf16[512,768]{1,0:T(8,128)(2,1)} %constant.4.clone.forward_hbm, ...), custom_call_target="tpu_custom_call" | custom-call | tf_op jit(solution)/shard_map/pallas_call | solution.py:407
  75.2 1.9 %copy.9 = bf16[64,4096]{1,0:T(8,128)(2,1)} copy(bf16[64,4096]{1,0:T(8,128)(2,1)} %shard_map.73) | data formatting | bytes 1048576

commit v4 on v2

--- a/solution.py
+++ b/solution.py
@@ -246,17 +246,12 @@
         return carry
 
     lax.fori_loop(1, peers, greet, 0)
-    loads[0].wait()
-    loads[1].wait()
-    signal[...] = key_ref[...].astype(jnp.float32) * value_ref[...].astype(jnp.float32)
-    for load in loads[2:]:
-        load.start()
     pl.semaphore_wait(barrier, peers - 1)
 
     my_rows = pl.ds(pl.multiple_of(me * rows, rows), rows)
     my_lanes = pl.ds(pl.multiple_of(me * LANES, LANES), LANES)
 
-    def send(step, carry):
+    def send(with_taps, with_signal, step, carry):
         turn = step // (seq_count * per_turn)
         inner = lax.rem(step, seq_count * per_turn)
         hop = inner // per_turn
@@ -268,32 +263,42 @@
 
         @pl.when(peer != me)
         def _():
-            pltpu.make_async_remote_copy(
-                src_ref=taps_hbm.at[:, lanes],
-                dst_ref=taps_in.at[my_rows, :],
-                send_sem=send_sem.at[1],
-                recv_sem=taps_sem.at[position],
-                device_id=(there, across),
-                device_id_type=MESH,
-            ).start()
-            pltpu.make_async_remote_copy(
-                src_ref=signal.at[:, lanes],
-                dst_ref=signal_in.at[my_rows, :],
-                send_sem=send_sem.at[0],
-                recv_sem=signal_sem.at[position],
-                device_id=(there, across),
-                device_id_type=MESH,
-            ).start()
+            if with_taps:
+                pltpu.make_async_remote_copy(
+                    src_ref=taps_hbm.at[:, lanes],
+                    dst_ref=taps_in.at[my_rows, :],
+                    send_sem=send_sem.at[1],
+                    recv_sem=taps_sem.at[position],
+                    device_id=(there, across),
+                    device_id_type=MESH,
+                ).start()
+            if with_signal:
+                pltpu.make_async_remote_copy(
+                    src_ref=signal.at[:, lanes],
+                    dst_ref=signal_in.at[my_rows, :],
+                    send_sem=send_sem.at[0],
+                    recv_sem=signal_sem.at[position],
+                    device_id=(there, across),
+                    device_id_type=MESH,
+                ).start()
 
         return carry
 
+    first = peers // turns
+    lax.fori_loop(0, first, functools.partial(send, True, False), 0)
+    loads[0].wait()
+    loads[1].wait()
+    signal[...] = key_ref[...].astype(jnp.float32) * value_ref[...].astype(jnp.float32)
+    for load in loads[2:]:
+        load.start()
     pltpu.make_async_copy(
         signal.at[:, my_lanes], signal_in.at[my_rows, :], signal_sem.at[position]
     ).start()
     pltpu.make_async_copy(
         taps_hbm.at[:, my_lanes], taps_in.at[my_rows, :], taps_sem.at[position]
     ).start()
-    lax.fori_loop(0, peers, send, 0)
+    lax.fori_loop(0, first, functools.partial(send, False, True), 0)
+    lax.fori_loop(first, peers, functools.partial(send, True, True), 0)
     for load in loads[2:]:
         load.wait()
 

time: 77.5 us -> 77.5 us (level)
  no operation moved by 1% of the time
where the time goes in v4:
time: 77.5 us; the launch traced here: 77.3 us
  Pallas kernels  75.5 us (97%)
  local copies, waits for them, and re-layouts  1.87 us (2%)
    pallas_call x1, Pallas kernels, fused_shards(): pl.pallas_call(functools.partial(conv_kernel, seq_count, group_count), ou...  75.5 us
    unnamed x1, local copies, waits for them, and re-layouts  1.87 us

profile of v4, /device:TPU:31, one launch (start us, length us, event | category | flops | bytes accessed | tf_op | source)
XLA Modules:
  0.0 77.3 jit_solution(16082163928604194299)
XLA Ops:
  0.0 75.5 %shard_map.73 = bf16[64,4096]{1,0:T(8,128)(2,1)} custom-call(bf16[64,4096]{1,0:T(8,128)(2,1)} %key_hbm.1, bf16[64,4096]{1,0:T(8,128)(2,1)} %value_hbm.1, f32[64,4096]{1,0:T(8,128)} %taps_hbm.1, bf16[64,4096]{1,0:T(8,128)(2,1)} %query_hbm.1, f32[1,4096]{1,0:T(1,128)} %bitcast.1, bf16[512,768]{1,0:T(8,128)(2,1)} %constant.4.clone.forward_hbm, ...), custom_call_target="tpu_custom_call" | custom-call | tf_op jit(solution)/shard_map/pallas_call | solution.py:402
  75.5 1.9 %copy.9 = bf16[64,4096]{1,0:T(8,128)(2,1)} copy(bf16[64,4096]{1,0:T(8,128)(2,1)} %shard_map.73) | data formatting | bytes 1048576
